TPU v7x, 32 devices: a whole 2x2x4 slice. The times are simulated.
32 devices in a mesh: depth: 8 (over y, x, core), seq: 4 (over z).
Axes of the slice: x: 2, y: 2, z: 4, core: 2. Of those that a mesh axis runs over, the one named last changes fastest.
Arguments:
- interfaces: bfloat16 [8, 1, 2048, 1024], P('depth', None, 'seq'), may hold values from -6 to 6
- doc_ids: int32 [1, 2048], replicated, may hold values from 0 to 3, never falling along the last dimension, each value on 1 to 1024 neighbouring positions
- w_attn: bfloat16 [8, 1, 4, 1024, 1024], P('depth'), may hold values from -0.1875 to 0.1875
- w_up: bfloat16 [8, 1, 1024, 4096], P('depth'), may hold values from -0.1875 to 0.1875
- w_down: bfloat16 [8, 1, 4096, 1024], P('depth'), may hold values from -0.09375 to 0.09375
- norm_gains: float32 [8, 1, 2, 1024], P('depth'), may hold values from 0.25 to 1.75
- coarse_gain: float32 [8, 1024], P('depth'), may hold values from 0 to 1
Outputs:
- relaxed: bfloat16 [8, 1, 2048, 1024], P('depth', None, 'seq')
Inputs may be any that keep to these rules, and one draw needn't show every extreme that they name: doc_ids never fall along a sequence and number the documents packed into it.
All inputs are finite; a program needn't handle non-finite values.
Results may differ from a plain program's by a relative error of at most 0.025.
Values may be sent and summed in bfloat16 or wider, within the bound.
No kernel may reach another device: no remote copies, remote signals or barrier semaphores. Data moves between devices by JAX's collectives and lax.ppermute only.
A program may use at most 192 MiB of HBM per device.

v0:
```python
import jax
import jax.numpy as jnp
from jax import lax
from jax.sharding import PartitionSpec as P

HEADS = 16


def passed_along(value, axis, steps):
    count = lax.axis_size(axis)
    first, last = (max(0, -steps), min(count, count - steps))
    return lax.ppermute(value, axis, [(source, source + steps) for source in range(first, last)])


def prefix_2(x, axis, join, neutral):
    place = lax.axis_index(axis)
    gathered = jax.tree.map(
        lambda a, kind: lax.all_gather(a.astype(kind), axis), x, (jnp.bfloat16, jnp.bfloat16)
    )
    state = jax.tree.map(lambda a, e: jnp.zeros_like(a) + jnp.asarray(e, a.dtype), x, neutral)

    def one(hop, state):
        return join(
            state,
            jax.tree.map(
                lambda a, own: lax.dynamic_index_in_dim(a, hop, 0, False).astype(own.dtype),
                gathered,
                x,
            ),
        )

    return lax.fori_loop(0, place, one, state)


def rms_norm(value_tensor, gain):
    return (
        value_tensor
        * lax.rsqrt(jnp.mean(value_tensor * value_tensor, axis=-1, keepdims=True) + 1e-05)
        * gain
    )


def one_layer(states, attn_w, up_w, lowering_matrix, gain_pair, doc_ids):
    batch, rows, width = states.shape
    head_dim = width // HEADS
    score_scale = head_dim ** (-0.5)
    normed = rms_norm(states.astype(jnp.float32), gain_pair[0]).astype(jnp.bfloat16)
    flat = normed.reshape(-1, width)
    queries = (
        jnp.dot(flat, attn_w[0], preferred_element_type=jnp.float32)
        .astype(jnp.bfloat16)
        .reshape(batch, rows, HEADS, head_dim)
    )
    my_seq = lax.axis_index("seq")
    query_pos = my_seq * rows + jnp.arange(rows, dtype=jnp.int32)
    query_doc = lax.dynamic_slice_in_dim(doc_ids, my_seq * rows, rows, 1)
    pieces = lax.all_gather(normed, "seq", axis=1, tiled=True)
    count_rows = pieces.shape[1]
    flat_piece = pieces.reshape(-1, width)
    key_rows = (
        jnp.dot(flat_piece, attn_w[1], preferred_element_type=jnp.float32)
        .astype(jnp.bfloat16)
        .reshape(batch, count_rows, width)
    )
    value_rows = (
        jnp.dot(flat_piece, attn_w[2], preferred_element_type=jnp.float32)
        .astype(jnp.bfloat16)
        .reshape(batch, count_rows, width)
    )
    width_keys = key_rows.shape[1]
    lookup_vectors_per_head = key_rows.reshape(batch, width_keys, HEADS, head_dim)
    value_heads = value_rows.reshape(batch, width_keys, HEADS, head_dim)
    scores = (
        jnp.einsum(
            "sqhd,skhd->shqk", queries, lookup_vectors_per_head, preferred_element_type=jnp.float32
        )
        * score_scale
    )
    key_pos = jnp.arange(width_keys, dtype=jnp.int32)
    allowed = (key_pos[None, :] <= query_pos[:, None])[None] & (
        query_doc[:, :, None] == doc_ids[:, None, :]
    )
    weights = jnp.where(allowed[:, None], jnp.exp(scores), jnp.zeros_like(scores))
    numerator = jnp.einsum(
        "shqk,skhd->shqd",
        weights.astype(jnp.bfloat16),
        value_heads,
        preferred_element_type=jnp.float32,
    )
    numerator, denominator = (numerator, jnp.sum(weights, axis=-1))
    attended = (
        (numerator / denominator[..., None])
        .transpose(0, 2, 1, 3)
        .reshape(batch * rows, width)
        .astype(jnp.bfloat16)
    )
    mixed = states.astype(jnp.float32) + jnp.dot(
        attended, attn_w[3], preferred_element_type=jnp.float32
    ).reshape(batch, rows, width)
    second = rms_norm(mixed, gain_pair[1]).astype(jnp.bfloat16).reshape(-1, width)
    expanded = jax.nn.gelu(jnp.dot(second, up_w, preferred_element_type=jnp.float32)).astype(
        jnp.bfloat16
    )
    result = mixed + jnp.dot(expanded, lowering_matrix, preferred_element_type=jnp.float32).reshape(
        batch, rows, width
    )
    return result.astype(jnp.bfloat16)


def run_section(states, doc_ids, w_attn, w_up, w_down, norm_gains):
    states = one_layer(states, w_attn[0, 0], w_up[0, 0], w_down[0, 0], norm_gains[0, 0], doc_ids)
    return states


def on_device(interfaces, doc_ids, w_attn, w_up, w_down, norm_gains, coarse_gain):
    following = passed_along(interfaces, "depth", -1)
    fine = run_section(interfaces[0], doc_ids, w_attn, w_up, w_down, norm_gains)
    mismatch = fine[None].astype(jnp.float32) - following.astype(jnp.float32)

    def compose(earlier, later):
        return (later[0] * earlier[0], later[0][:, None, None, :] * earlier[1] + later[1])

    identity_map = (jnp.ones_like(coarse_gain), jnp.zeros_like(mismatch))
    prefix = prefix_2((coarse_gain, mismatch), "depth", compose, identity_map)
    correction = prefix[1]
    corrected = (interfaces.astype(jnp.float32) + correction).astype(jnp.bfloat16)
    relaxed = run_section(corrected[0], doc_ids, w_attn, w_up, w_down, norm_gains)
    return relaxed[None]


def solution(mesh):
    in_specs = (
        P("depth", None, "seq", None),
        P(),
        P("depth", None, None, None, None),
        P("depth", None, None, None),
        P("depth", None, None, None),
        P("depth", None, None, None),
        P("depth", None),
    )
    out_specs = P("depth", None, "seq", None)
    return jax.shard_map(
        on_device, mesh=mesh, in_specs=in_specs, out_specs=out_specs, check_vma=False
    )
```

profile of v0, /device:TPU:8, one launch (start us, length us, event | category | flops | bytes accessed | tf_op | source)
XLA Modules:
  0.0 442.7 jit_solution(6891310717222821001)
XLA Ops:
  6.5 0.0 copy-start
  6.5 0.0 all-gather.7.cloned.1.call-start
  6.5 0.8 fusion.184
  7.4 1.5 fusion.75
  8.9 2.5 fusion.77
  11.4 0.0 all-gather.7.cloned.1.call-update
  11.4 0.0 all-gather.11.cloned.1.call-start
  11.4 0.0 copy-done
  11.5 1.3 collective-permute-start
  12.8 0.0 copy-start.5
  12.8 2.9 fusion.125
  15.7 0.5 copy.14
  16.3 0.0 copy-done.5
  16.3 1.0 fusion.50
  17.3 0.0 copy-start.3
  17.3 73.5 %all-gather.7.cloned.1.call-done = bf16[1,2048,1024]{2,1,0:T(8,128)(2,1)} async-done(((bf16[1,512,1024]{2,1,0:T(8,128)(2,1)}), bf16[1,2048,1024]{2,1,0:T(8,128)(2,1)}) %all-gather.7.cloned.1.call-update) | async-done | bytes 4194320 | tf_op jit(solution)/shard_map/all_gather | solution.py:57
  90.8 9.4 %fusion.51 = bf16[2048,1024]{0,1:T(8,128)(2,1)} fusion(bf16[1,2048,1024]{2,1,0:T(8,128)(2,1)} %all-gather.7.cloned.1.call-done, bf16[1,1,4,1024,1024]{4,3,2,1,0:T(8,128)(2,1)} %param.11), kind=kOutput, calls=%fused_computation.54 | convolution fusion | flops 4297064448 | bytes 10485760 | tf_op jit(solution)/shard_map/dot_general | solution.py:61
  100.2 0.0 copy-start.7
  100.2 27.8 %fusion = (f32[16,512]{1,0:T(8,128)S(1)}, f32[16,512,2048]{2,1,0:T(8,128)}) fusion(pred[512,2048]{1,0:T(8,128)(4,1)S(1)} %fusion.50, bf16[512,16,64]{0,2,1:T(8,128)(2,1)S(1)} %bitcast.175, bf16[2048,16,64]{0,2,1:T(8,128)(2,1)} %bitcast.188), kind=kOutput, calls=%fused_computation.4 | convolution fusion | flops 2197807104 | bytes 73433088 | tf_op jit(solution)/shard_map/sqhd,skhd->shqk/dot_general | solution.py:74
  128.0 0.0 copy-done.7
  128.0 19.0 %fusion.54 = bf16[2048,1024]{0,1:T(8,128)(2,1)} fusion(bf16[1,2048,1024]{2,1,0:T(8,128)(2,1)S(1)} %copy-done.7, bf16[1,1,4,1024,1024]{4,3,2,1,0:T(8,128)(2,1)} %param.11), kind=kOutput, calls=%fused_computation.55 | convolution fusion | flops 4297064448 | bytes 10485760 | tf_op jit(solution)/shard_map/dot_general | solution.py:66
  147.1 0.0 copy-done.3
  147.1 24.7 %divide_convert_fusion.1 = bf16[16,512,64]{1,2,0:T(8,128)(2,1)S(1)} fusion(bf16[2048,16,64]{0,2,1:T(8,128)(2,1)} %bitcast.187, f32[16,512,2048]{2,1,0:T(8,128)} %get-tuple-element.80, pred[512,2048]{1,0:T(8,128)(4,1)S(1)} %fusion.50, f32[16,512]{1,0:T(8,128)S(1)} %get-tuple-element.79), kind=kOutput, calls=%fused_computation.103 | convolution fusion | flops 2198863872 | bytes 73433088 | tf_op jit(solution)/shard_map/shqk,skhd->shqd/dot_general | solution.py:84
  171.7 4.2 multiply_reduce_fusion.1
  176.0 0.0 collective-permute-done
  176.0 0.0 copy-start.6
  176.0 17.2 %fusion.88 = bf16[1,1,512,1024]{3,2,1,0:T(8,128)(2,1)} fusion(bf16[1,1,512,1024]{3,2,1,0:T(8,128)(2,1)} %collective-permute-done, f32[512,1024]{1,0:T(8,128)} %get-tuple-element.82, bf16[1,1,4096,1024]{3,2,1,0:T(8,128)(2,1)} %param.13, bf16[1,1,1024,4096]{3,2,1,0:T(8,128)(2,1)} %param.12, f32[1024]{0:T(1024)S(1)} %bitcast.184, f32[512]{0:T(512)S(1)} %add_rsqrt_fusion.2), kind=kOutput, calls=%fused_computation.83 | convolution fusion | flops 8613527552 | bytes 20977664 | tf_op jit(solution)/shard_map/dot_general | solution.py:104
  193.2 0.0 all-gather.11.cloned.1.call-update
  193.3 0.0 all-gather.9.cloned.1.call-start
  193.3 0.0 copy-done.6
  193.3 9.2 %all-gather.2 = bf16[8,1,1024]{2,1,0:T(2,128)(2,1)S(1)} all-gather(bf16[1,1,1024]{2,1,0:T(2,128)(2,1)S(1)} %convert_bitcast_fusion.4), channel_id=2, replica_groups=mesh['depth'=8,'seq'=4] {'depth'}, dimensions={0}, use_global_device_ids=true | all-gather | bytes 18432 | tf_op jit(solution)/shard_map/all_gather | solution.py:18
  202.6 46.4 %all-gather.11.cloned.1.call-done = bf16[8,1,512,1024]{3,2,1,0:T(8,128)(2,1)} async-done(((bf16[1,1,512,1024]{3,2,1,0:T(8,128)(2,1)}), bf16[8,1,512,1024]{3,2,1,0:T(8,128)(2,1)}) %all-gather.11.cloned.1.call-update) | async-done | bytes 8388624 | tf_op jit(solution)/shard_map/all_gather | solution.py:18
  249.0 0.2 broadcast_in_dim.16
  249.2 0.4 fusion.78
  249.6 0.0 copy-start.1
  249.7 1.0 copy-done.1
  250.6 1.3 fusion.80
  251.9 0.0 all-gather.9.cloned.1.call-update
  251.9 3.2 fusion.128
  255.1 0.9 copy.16
  256.1 0.0 copy-start.4
  256.1 88.8 %all-gather.9.cloned.1.call-done = bf16[1,2048,1024]{2,1,0:T(8,128)(2,1)} async-done(((bf16[1,512,1024]{2,1,0:T(8,128)(2,1)}), bf16[1,2048,1024]{2,1,0:T(8,128)(2,1)}) %all-gather.9.cloned.1.call-update) | async-done | bytes 4194320 | tf_op jit(solution)/shard_map/all_gather | solution.py:57
  344.9 9.4 %fusion.57 = bf16[2048,1024]{0,1:T(8,128)(2,1)} fusion(bf16[1,2048,1024]{2,1,0:T(8,128)(2,1)} %all-gather.9.cloned.1.call-done, bf16[1,1,4,1024,1024]{4,3,2,1,0:T(8,128)(2,1)} %param.11), kind=kOutput, calls=%fused_computation.56 | convolution fusion | flops 4297064448 | bytes 10485760 | tf_op jit(solution)/shard_map/dot_general | solution.py:61
  354.3 0.0 copy-done.4
  354.3 0.0 copy-start.8
  354.3 27.8 %fusion.2 = (f32[16,512]{1,0:T(8,128)S(1)}, f32[16,512,2048]{2,1,0:T(8,128)}) fusion(pred[512,2048]{1,0:T(8,128)(4,1)S(1)} %copy-done.4, bf16[512,16,64]{0,2,1:T(8,128)(2,1)S(1)} %bitcast.176, bf16[2048,16,64]{0,2,1:T(8,128)(2,1)} %bitcast.189), kind=kOutput, calls=%fused_computation.6 | convolution fusion | flops 2197807104 | bytes 73433088 | tf_op jit(solution)/shard_map/sqhd,skhd->shqk/dot_general | solution.py:74
  382.1 0.0 copy-done.8
  382.1 7.8 %fusion.60 = bf16[2048,1024]{0,1:T(8,128)(2,1)} fusion(bf16[1,2048,1024]{2,1,0:T(8,128)(2,1)S(1)} %copy-done.8, bf16[1,1,4,1024,1024]{4,3,2,1,0:T(8,128)(2,1)} %param.11), kind=kOutput, calls=%fused_computation.57 | convolution fusion | flops 4297064448 | bytes 10485760 | tf_op jit(solution)/shard_map/dot_general | solution.py:66
  389.9 0.0 copy-start.2
  389.9 24.9 %divide_convert_fusion = bf16[16,512,64]{1,2,0:T(8,128)(2,1)S(1)} fusion(bf16[2048,16,64]{0,2,1:T(8,128)(2,1)} %bitcast.186, f32[16,512,2048]{2,1,0:T(8,128)} %get-tuple-element.84, pred[512,2048]{1,0:T(8,128)(4,1)S(1)} %copy-done.4, f32[16,512]{1,0:T(8,128)S(1)} %get-tuple-element.83), kind=kOutput, calls=%fused_computation.99 | convolution fusion | flops 2198863872 | bytes 73433088 | tf_op jit(solution)/shard_map/shqk,skhd->shqd/dot_general | solution.py:84
  414.8 0.0 copy-done.2
  414.8 4.2 multiply_reduce_fusion
  419.1 16.9 %fusion.138 = bf16[1,1,512,1024]{3,2,1,0:T(8,128)(2,1)} fusion(f32[512,1024]{1,0:T(8,128)} %get-tuple-element.86, bf16[1,1,4096,1024]{3,2,1,0:T(8,128)(2,1)} %param.13, bf16[1,1,1024,4096]{3,2,1,0:T(8,128)(2,1)} %param.12, f32[512]{0:T(512)S(1)} %add_rsqrt_fusion, f32[1024]{0:T(1024)S(1)} %bitcast.185), kind=kOutput, calls=%fused_computation.115 | convolution fusion | flops 8611430400 | bytes 19929088 | tf_op jit(solution)/shard_map/dot_general | solution.py:104
  (8 shorter events, 0.1 us)
Async XLA Ops:
  6.5 4.9 %copy-start = (bf16[1,1,512,1024]{3,2,1,0:T(8,128)(2,1)S(1)}, bf16[1,1,512,1024]{3,2,1,0:T(8,128)(2,1)}, u32[]{:S(2)}) copy-start(bf16[1,1,512,1024]{3,2,1,0:T(8,128)(2,1)} %param.9) | copy-start | bytes 3145732
  6.5 84.3 %all-gather.7.cloned.1.call-start = ((), (), s32[]{:S(2)}) async-start(), calls=%async_computation | async-start | bytes 5242880 | tf_op jit(solution)/shard_map/all_gather | solution.py:57
  11.4 237.6 %all-gather.11.cloned.1.call-start = ((), (), s32[]{:S(2)}) async-start(), calls=%async_computation.2 | async-start | bytes 9437184 | tf_op jit(solution)/shard_map/all_gather | solution.py:18
  11.5 164.5 %collective-permute-start = (bf16[1,1,512,1024]{3,2,1,0:T(8,128)(2,1)S(1)}, bf16[1,1,512,1024]{3,2,1,0:T(8,128)(2,1)}, u32[]{:S(2)}, u32[]{:S(2)}) collective-permute-start(bf16[1,1,512,1024]{3,2,1,0:T(8,128)(2,1)S(1)} %copy-done), channel_id=1, source_target_pairs={{4,0},{8,4},{12,8},{16,12},{20,16},{24,20},{28,24},{5,1},{9,5},{13... | collective-permute-start | bytes 3145736 | tf_op jit(solution)/shard_map/ppermute | solution.py:12
  12.8 3.5 copy-start.5
  17.3 129.8 %copy-start.3 = (pred[512,2048]{1,0:T(8,128)(4,1)}, pred[512,2048]{1,0:T(8,128)(4,1)S(1)}, u32[]{:S(2)}) copy-start(pred[512,2048]{1,0:T(8,128)(4,1)S(1)} %fusion.50) | copy-start | bytes 3145732
  100.2 27.8 %copy-start.7 = (bf16[1,2048,1024]{2,1,0:T(8,128)(2,1)S(1)}, bf16[1,2048,1024]{2,1,0:T(8,128)(2,1)}, u32[]{:S(2)}) copy-start(bf16[1,2048,1024]{2,1,0:T(8,128)(2,1)} %all-gather.7.cloned.1.call-done) | copy-start | bytes 12582916
  176.0 17.3 %copy-start.6 = (f32[1,1024]{1,0:T(1,128)S(1)}, f32[1,1024]{1,0:T(1,128)}, u32[]{:S(2)}) copy-start(f32[1,1024]{1,0:T(1,128)} %param.15) | copy-start | bytes 12292
  193.3 151.6 %all-gather.9.cloned.1.call-start = ((), (), s32[]{:S(2)}) async-start(), calls=%async_computation.1 | async-start | bytes 5242880 | tf_op jit(solution)/shard_map/all_gather | solution.py:57
  249.6 1.0 copy-start.1
  256.1 98.2 %copy-start.4 = (pred[512,2048]{1,0:T(8,128)(4,1)S(1)}, pred[512,2048]{1,0:T(8,128)(4,1)}, u32[]{:S(2)}) copy-start(pred[512,2048]{1,0:T(8,128)(4,1)} %copy-done.3) | copy-start | bytes 3145732
  354.3 27.8 %copy-start.8 = (bf16[1,2048,1024]{2,1,0:T(8,128)(2,1)S(1)}, bf16[1,2048,1024]{2,1,0:T(8,128)(2,1)}, u32[]{:S(2)}) copy-start(bf16[1,2048,1024]{2,1,0:T(8,128)(2,1)} %all-gather.9.cloned.1.call-done) | copy-start | bytes 12582916
  389.9 24.9 %copy-start.2 = (bf16[1,1,512,1024]{3,2,1,0:T(8,128)(2,1)S(1)}, bf16[1,1,512,1024]{3,2,1,0:T(8,128)(2,1)}, u32[]{:S(2)}) copy-start(bf16[1,1,512,1024]{3,2,1,0:T(8,128)(2,1)} %copy-done.1) | copy-start | bytes 3145732
Sparse Core Ops, SparseCore 0:
  11.5 79.2 all-gather.6
  193.4 55.5 all-gather.10
  252.0 92.7 all-gather.8
where the time goes:
time: 450 us; the launch traced here: 443 us
  waiting for transfers between devices  209 us (46%)
  matrix products  200 us (44%)
  between operations  13.5 us (3%)
  blocking collectives  9.23 us (2%)
  other arithmetic  6.72 us (1%)
    all_gather x2, waiting for transfers between devices, one_layer(): pieces = lax.all_gather(normed, 'seq', axis=1, tiled=True)  162 us
    dot_general x2, matrix products, one_layer(): jnp.einsum('sqhd,skhd->shqk', queries, lookup_vectors_per_head, preferred...  55.6 us
    dot_general x2, matrix products, one_layer(): jnp.einsum('shqk,skhd->shqd', weights.astype(jnp.bfloat16), value_heads,...  49.6 us
    all_gather x1, waiting for transfers between devices, prefix_2(): lax.all_gather(a.astype(kind), axis)  46.4 us
    dot_general x2, matrix products, one_layer(): jnp.dot(expanded, lowering_matrix, preferred_element_type=jnp.float32)  34.2 us
    dot_general x2, matrix products, one_layer(): jnp.dot(flat_piece, attn_w[2], preferred_element_type=jnp.float32)  26.9 us
    dot_general x2, matrix products, one_layer(): jnp.dot(flat_piece, attn_w[1], preferred_element_type=jnp.float32)  18.8 us
    all_gather x1, blocking collectives, prefix_2(): lax.all_gather(a.astype(kind), axis)  9.23 us
  transfers between devices with their start and end apart: 4, of which 3 were waited for; matrix products, arithmetic and copies ran while one was open for 21% of the time, Pallas kernels for 0%

commit v1 on v0

v1 whole, which is shorter than its diff:
```python
import functools

import jax
import jax.numpy as jnp
from jax import lax
from jax.experimental import pallas as pl
from jax.experimental.pallas import tpu as pltpu
from jax.sharding import PartitionSpec as P

HEADS = 16
LANES = 128
BLOCK = 256
VMEM_BYTES = 48 * 1024 * 1024
F32 = jnp.float32
BF16 = jnp.bfloat16


def rms_norm(value, gain):
    return value * lax.rsqrt(jnp.mean(value * value, axis=-1, keepdims=True) + 1e-05) * gain


def dot(a, b):
    return jnp.dot(a, b, preferred_element_type=F32)


def attend(q_ref, k_ref, v_ref, num_ref, den_ref, qcol_ref, krow_ref, qdoc_ref, kdoc_ref, causal):
    rows, width = q_ref.shape
    keys = k_ref.shape[0]
    head_dim = width // HEADS
    q_block, k_block = min(BLOCK, rows), min(BLOCK, keys)
    lane = lax.broadcasted_iota(jnp.int32, (1, LANES), 1)
    members = [lane // head_dim == i for i in range(LANES // head_dim)]
    count_q, count_k = rows // q_block, keys // k_block

    def one(index, carry):
        qi, ki = index // count_k, index % count_k
        q0 = pl.multiple_of(qi * q_block, q_block)
        k0 = pl.multiple_of(ki * k_block, k_block)
        needed = kdoc_ref[0, k0 + k_block - 1] >= qdoc_ref[0, q0]
        if causal:
            needed = (k0 <= q0) & (needed | (k0 == q0))

        @pl.when(needed)
        def _():
            allowed = qcol_ref[pl.ds(q0, q_block), :1] == krow_ref[:, pl.ds(k0, k_block)]
            if causal:
                q_pos = q0 + lax.broadcasted_iota(jnp.int32, (q_block, k_block), 0)
                k_pos = k0 + lax.broadcasted_iota(jnp.int32, (q_block, k_block), 1)
                allowed = allowed & (k_pos <= q_pos)
            ones = jnp.ones((k_block, LANES), BF16)
            for pair in range(width // LANES):
                cols = slice(pair * LANES, (pair + 1) * LANES)
                queries = q_ref[pl.ds(q0, q_block), cols]
                keys_here = k_ref[pl.ds(k0, k_block), cols]
                values = jnp.concatenate([v_ref[pl.ds(k0, k_block), cols], ones], axis=1)
                num, den = None, None
                for member in members:
                    scores = lax.dot_general(
                        jnp.where(member, queries, jnp.zeros_like(queries)),
                        keys_here,
                        (((1,), (1,)), ((), ())),
                        preferred_element_type=F32,
                    )
                    weights = jnp.where(allowed, jnp.exp(scores), 0.0).astype(BF16)
                    out = dot(weights, values)
                    if num is None:
                        num, den = out[:, :LANES], out[:, LANES:]
                    else:
                        num = jnp.where(member, out[:, :LANES], num)
                        den = jnp.where(member, out[:, LANES:], den)
                num_ref[pl.ds(q0, q_block), cols] += num
                den_ref[pl.ds(q0, q_block), cols] += den

        return carry

    lax.fori_loop(0, count_q * count_k, one, 0)


def own_kernel(x_ref, gain_ref, w_ref, qcol_ref, krow_ref, doc_ref, q_ref, num_ref, den_ref, n_ref, k_ref, v_ref):
    step = pl.program_id(0)
    head_dim = x_ref.shape[1] // HEADS

    @pl.when(step == 0)
    def _():
        n_ref[...] = rms_norm(x_ref[...].astype(F32), gain_ref[0:1]).astype(BF16)
        q_ref[...] = dot(n_ref[...], w_ref[...]).astype(BF16) * jnp.asarray(head_dim ** (-0.5), BF16)

    @pl.when(step == 1)
    def _():
        k_ref[...] = dot(n_ref[...], w_ref[...]).astype(BF16)

    @pl.when(step == 2)
    def _():
        v_ref[...] = dot(n_ref[...], w_ref[...]).astype(BF16)
        num_ref[...] = jnp.zeros_like(num_ref)
        den_ref[...] = jnp.zeros_like(den_ref)
        attend(q_ref, k_ref, v_ref, num_ref, den_ref, qcol_ref, krow_ref, doc_ref, doc_ref, True)


def piece_kernel(
    x_ref, gain_ref, w_ref, q_ref, num_in, den_in, qcol_ref, krow_ref, qdoc_ref, kdoc_ref,
    num_ref, den_ref, n_ref, k_ref, v_ref,
):
    step = pl.program_id(0)
    needed = kdoc_ref[0, kdoc_ref.shape[1] - 1] >= qdoc_ref[0, 0]

    @pl.when(needed & (step == 0))
    def _():
        n_ref[...] = rms_norm(x_ref[...].astype(F32), gain_ref[0:1]).astype(BF16)
        k_ref[...] = dot(n_ref[...], w_ref[...]).astype(BF16)

    @pl.when(step == 1)
    def _():
        num_ref[...] = num_in[...]
        den_ref[...] = den_in[...]

    @pl.when(needed & (step == 1))
    def _():
        v_ref[...] = dot(n_ref[...], w_ref[...]).astype(BF16)
        attend(q_ref, k_ref, v_ref, num_ref, den_ref, qcol_ref, krow_ref, qdoc_ref, kdoc_ref, False)


def finish_kernel(x_ref, num_ref, den_ref, wo_ref, gain_ref, up_ref, down_ref, out_ref, acc_ref, n_ref):
    step = pl.program_id(0)

    @pl.when(step == 0)
    def _():
        attended = (num_ref[...] / den_ref[...]).astype(BF16)
        mixed = x_ref[...].astype(F32) + dot(attended, wo_ref[...])
        acc_ref[...] = mixed
        n_ref[...] = rms_norm(mixed, gain_ref[1:2]).astype(BF16)

    expanded = jax.nn.gelu(dot(n_ref[...], up_ref[...])).astype(BF16)
    acc_ref[...] += dot(expanded, down_ref[...])

    @pl.when(step == pl.num_programs(0) - 1)
    def _():
        out_ref[...] = acc_ref[...].astype(BF16)


def whole(shape):
    return pl.BlockSpec(shape, lambda *_: (0,) * len(shape))


def smem():
    return pl.BlockSpec(memory_space=pltpu.SMEM)


def params():
    return pltpu.CompilerParams(vmem_limit_bytes=VMEM_BYTES, dimension_semantics=("arbitrary",))


def own_part(x, gains, w_attn, qcol, doc):
    rows, width = x.shape
    return pl.pallas_call(
        own_kernel,
        grid=(3,),
        in_specs=[
            whole((rows, width)),
            whole(gains.shape),
            pl.BlockSpec((None, width, width), lambda i: (i, 0, 0)),
            whole((rows, LANES)),
            whole((1, rows)),
            smem(),
        ],
        out_specs=[whole((rows, width))] * 3,
        out_shape=[
            jax.ShapeDtypeStruct((rows, width), BF16),
            jax.ShapeDtypeStruct((rows, width), F32),
            jax.ShapeDtypeStruct((rows, width), F32),
        ],
        scratch_shapes=[pltpu.VMEM((rows, width), BF16)] * 3,
        compiler_params=params(),
        cost_estimate=pl.CostEstimate(
            flops=6 * rows * width * width + 16 * rows * rows * width,
            bytes_accessed=6 * width * width + 12 * rows * width,
            transcendentals=HEADS * rows * rows,
        ),
        name="own_part",
    )(x, gains, w_attn, qcol, doc, doc)


def piece_part(x, gains, w_attn, q, num, den, qcol, qdoc, kdoc):
    rows, width = q.shape
    keys = x.shape[0]
    return pl.pallas_call(
        piece_kernel,
        grid=(2,),
        in_specs=[
            whole((keys, width)),
            whole(gains.shape),
            pl.BlockSpec((None, width, width), lambda i: (i + 1, 0, 0)),
            whole((rows, width)),
            whole((rows, width)),
            whole((rows, width)),
            whole((rows, LANES)),
            whole((1, keys)),
            smem(),
            smem(),
        ],
        out_specs=[whole((rows, width))] * 2,
        out_shape=[jax.ShapeDtypeStruct((rows, width), F32)] * 2,
        scratch_shapes=[pltpu.VMEM((keys, width), BF16)] * 3,
        input_output_aliases={4: 0, 5: 1},
        compiler_params=params(),
        cost_estimate=pl.CostEstimate(
            flops=4 * keys * width * width + 16 * rows * keys * width,
            bytes_accessed=4 * width * width + 20 * rows * width,
            transcendentals=HEADS * rows * keys,
        ),
        name="piece_part",
    )(x, gains, w_attn, q, num, den, qcol, kdoc, qdoc, kdoc)


def finish_part(x, num, den, w_attn, gains, w_up, w_down):
    rows, width = x.shape
    hidden = w_up.shape[1]
    tile = min(512, hidden)
    return pl.pallas_call(
        finish_kernel,
        grid=(hidden // tile,),
        in_specs=[
            whole((rows, width)),
            whole((rows, width)),
            whole((rows, width)),
            pl.BlockSpec((None, width, width), lambda i: (3, 0, 0)),
            whole(gains.shape),
            pl.BlockSpec((width, tile), lambda i: (0, i)),
            pl.BlockSpec((tile, width), lambda i: (i, 0)),
        ],
        out_specs=whole((rows, width)),
        out_shape=jax.ShapeDtypeStruct((rows, width), BF16),
        scratch_shapes=[pltpu.VMEM((rows, width), F32), pltpu.VMEM((rows, width), BF16)],
        compiler_params=params(),
        cost_estimate=pl.CostEstimate(
            flops=2 * rows * width * width + 4 * rows * width * hidden,
            bytes_accessed=2 * width * width + 4 * width * hidden + 12 * rows * width,
            transcendentals=rows * hidden,
        ),
        name="finish_part",
    )(x, num, den, w_attn, gains, w_up, w_down)


def shifted(value, axis, steps):
    count = lax.axis_size(axis)
    first, last = max(0, -steps), min(count, count - steps)
    return lax.ppermute(value, axis, [(i, i + steps) for i in range(first, last)])


def swapped(value, axis, bit):
    return lax.ppermute(value, axis, [(i, i ^ bit) for i in range(lax.axis_size(axis))])


def section(x, docs, hops, w_attn, w_up, w_down, gains):
    qcol, doc_pieces = docs
    qdoc = doc_pieces[0]
    piece = shifted(x, "seq", 1) if hops else None
    q, num, den = own_part(x, gains, w_attn, qcol, qdoc)
    for hop in range(1, hops + 1):
        here = piece
        if hop < hops:
            piece = shifted(here, "seq", 1)
        num, den = piece_part(here, gains, w_attn, q, num, den, qcol, qdoc, doc_pieces[hop])
    return finish_part(x, num, den, w_attn, gains, w_up, w_down)


def corrections(fine, following, gain):
    count = lax.axis_size("depth")
    place = lax.axis_index("depth")
    rows = fine.shape[0]
    half = rows // 2
    odd = place % 2 == 1
    mismatch = fine.astype(F32) - following.astype(F32)
    low, high = mismatch[:half], mismatch[half:]
    mine = jnp.where(odd, high, low)
    other = swapped(jnp.where(odd, low, high).astype(BF16), "depth", 1).astype(F32)
    m_even, m_odd = jnp.where(odd, other, mine), jnp.where(odd, mine, other)
    gain_other = swapped(gain, "depth", 1)
    g_even, g_odd = jnp.where(odd, gain_other, gain), jnp.where(odd, gain, gain_other)
    total, factor = g_odd * m_even + m_odd, g_even * g_odd
    before, factor_before = jnp.zeros_like(total), jnp.ones_like(factor)
    bit = 2
    while bit < count:
        upper = (place // bit) % 2 == 1
        if 2 * bit < count:
            theirs = swapped(total.astype(BF16), "depth", bit).astype(F32)
            their_factor = swapped(factor, "depth", bit)
            total_next = jnp.where(upper, factor * theirs + total, their_factor * total + theirs)
            factor_next = factor * their_factor
        else:
            theirs = lax.ppermute(
                total.astype(BF16), "depth", [(i, i + bit) for i in range(count) if not i & bit]
            ).astype(F32)
            their_factor = factor
            total_next, factor_next = total, factor
        before = jnp.where(upper, factor_before * theirs + before, before)
        factor_before = jnp.where(upper, factor_before * their_factor, factor_before)
        total, factor = total_next, factor_next
        bit *= 2
    c_even, c_odd = before, g_even * before + m_even
    mine = jnp.where(odd, c_odd, c_even)
    other = swapped(jnp.where(odd, c_even, c_odd).astype(BF16), "depth", 1).astype(F32)
    return jnp.concatenate([jnp.where(odd, other, mine), jnp.where(odd, mine, other)], axis=0)


def on_device(interfaces, doc_ids, w_attn, w_up, w_down, norm_gains, coarse_gain):
    rows = interfaces.shape[2]
    length = doc_ids.shape[1]
    longest = length // 2
    hops = min(lax.axis_size("seq") - 1, -(-(longest - 1) // rows))
    my_seq = lax.axis_index("seq")
    x = interfaces[0, 0]
    following = shifted(x, "depth", -1)

    def doc_piece(hop):
        start = (my_seq - hop) * rows
        ids = lax.dynamic_slice_in_dim(doc_ids, jnp.maximum(start, 0), rows, 1)
        return jnp.where(start >= 0, ids, -1)

    doc_pieces = [doc_piece(hop) for hop in range(hops + 1)]
    qcol = jnp.broadcast_to(doc_pieces[0].reshape(rows, 1), (rows, LANES))
    layer = functools.partial(
        section,
        docs=(qcol, doc_pieces),
        hops=hops,
        w_attn=w_attn[0, 0],
        w_up=w_up[0, 0],
        w_down=w_down[0, 0],
        gains=norm_gains[0, 0],
    )
    fine = layer(x)
    correction = corrections(fine, following, coarse_gain)
    corrected = (x.astype(F32) + correction).astype(BF16)
    return layer(corrected)[None, None]


def solution(mesh):
    in_specs = (
        P("depth", None, "seq", None),
        P(),
        P("depth", None, None, None, None),
        P("depth", None, None, None),
        P("depth", None, None, None),
        P("depth", None, None, None),
        P("depth", None),
    )
    out_specs = P("depth", None, "seq", None)
    return jax.shard_map(
        on_device, mesh=mesh, in_specs=in_specs, out_specs=out_specs, check_vma=False
    )
```

time: 450 us -> 198 us (0.44); the launches traced: 443 us -> 197 us
  matrix products: 200 us -> 0 us
  waiting for transfers between devices: 209 us -> 69.7 us
  Pallas kernels: 0 us -> 90.8 us
  starting transfers between devices: 1.38 us -> 25.1 us
  between operations: 13.5 us -> 0.19 us
  blocking collectives: 9.23 us -> 0 us
    all_gather x3 -> x0, waiting for transfers between devices: 209 us -> none  [the longest x2 162 us: one_layer(): pieces = lax.all_gather(normed, 'seq', axis=1, tiled=True)]
    dot_general x14 -> x0, matrix products: 200 us -> none  [the longest x2 55.6 us: one_layer(): jnp.einsum('sqhd,skhd->shqk', queries, lookup_vectors_per_head, preferred...]
    pallas_call x0 -> x8, Pallas kernels: none -> 90.8 us  [the longest x4 34.2 us: piece_part(): pl.pallas_call(piece_kernel, grid=(2,), in_specs=[whole((keys, width)), w...]
    ppermute x1 -> x11, waiting for transfers between devices: 0.01 us -> 69.7 us  [the longest x5 44 us: shifted(): lax.ppermute(value, axis, [(i, i + steps) for i in range(first, last)])]
    ppermute x1 -> x11, starting transfers between devices: 1.29 us -> 25.1 us  [the longest x5 18.3 us: shifted(): lax.ppermute(value, axis, [(i, i + steps) for i in range(first, last)])]
    all_gather x1 -> x0, blocking collectives: 9.23 us -> none  [prefix_2(): lax.all_gather(a.astype(kind), axis)]
  transfers between devices with their start and end apart: 4 -> 11, of which waited for: 3 -> 6; matrix products, arithmetic and copies ran while one was open for 21% -> 1% of each run, Pallas kernels for 0% -> 35%
where the time goes in v1:
time: 198 us; the launch traced here: 197 us
  Pallas kernels  90.8 us (46%)
  waiting for transfers between devices  69.7 us (35%)
  starting transfers between devices  25.1 us (13%)
  other arithmetic  7.11 us (4%)
  local copies, waits for them, and re-layouts  3.74 us (2%)
    ppermute x5, waiting for transfers between devices, shifted(): lax.ppermute(value, axis, [(i, i + steps) for i in range(first, last)])  44 us
    pallas_call x4, Pallas kernels, piece_part(): pl.pallas_call(piece_kernel, grid=(2,), in_specs=[whole((keys, width)), w...  34.2 us
    pallas_call x2, Pallas kernels, finish_part(): pl.pallas_call(finish_kernel, grid=(hidden // tile,), in_specs=[whole((ro...  33.1 us
    pallas_call x2, Pallas kernels, own_part(): pl.pallas_call(own_kernel, grid=(3,), in_specs=[whole((rows, width)), who...  23.6 us
    ppermute x5, starting transfers between devices, shifted(): lax.ppermute(value, axis, [(i, i + steps) for i in range(first, last)])  18.3 us
    ppermute x5, waiting for transfers between devices, swapped(): lax.ppermute(value, axis, [(i, i ^ bit) for i in range(lax.axis_size(axis...  15.5 us
    ppermute x1, waiting for transfers between devices, corrections(): lax.ppermute(total.astype(BF16), 'depth', [(i, i + bit) for i in range(co...  10.1 us
    ppermute x1, starting transfers between devices, corrections(): lax.ppermute(total.astype(BF16), 'depth', [(i, i + bit) for i in range(co...  4.22 us
  transfers between devices with their start and end apart: 11, of which 6 were waited for; matrix products, arithmetic and copies ran while one was open for 1% of the time, Pallas kernels for 35%

profile of v1, /device:TPU:8, one launch (start us, length us, event | category | flops | bytes accessed | tf_op | source)
XLA Modules:
  0.0 196.6 jit_solution(11777786414261789998)
XLA Ops:
  0.0 3.5 %collective-permute-start.2 = (bf16[512,1024]{1,0:T(8,128)(2,1)}, bf16[512,1024]{1,0:T(8,128)(2,1)S(1)}, u32[]{:S(2)}, u32[]{:S(2)}) collective-permute-start(bf16[512,1024]{1,0:T(8,128)(2,1)} %bitcast.13), channel_id=1, source_target_pairs={{0,1},{1,2},{2,3},{4,5},{5,6},{6,7},{8,9},{9,10},{10,11},{12,13},{... | collective-permute-start | bytes 3145736 | tf_op jit(solution)/shard_map/ppermute | solution.py:247
  3.5 1.3 collective-permute-start.4
  4.8 0.9 broadcast_select_fusion.3
  5.7 21.3 %collective-permute-done.2.x_ref = bf16[512,1024]{1,0:T(8,128)(2,1)S(1)} collective-permute-done((bf16[512,1024]{1,0:T(8,128)(2,1)}, bf16[512,1024]{1,0:T(8,128)(2,1)S(1)}, u32[]{:S(2)}, u32[]{:S(2)}) %collective-permute-start.2) | collective-permute-done | bytes 1048608 | tf_op jit(solution)/shard_map/ppermute | solution.py:247
  27.0 3.5 %collective-permute-start.3 = (bf16[512,1024]{1,0:T(8,128)(2,1)S(1)}, bf16[512,1024]{1,0:T(8,128)(2,1)S(1)}, u32[]{:S(2)}, u32[]{:S(2)}) collective-permute-start(bf16[512,1024]{1,0:T(8,128)(2,1)S(1)} %collective-permute-done.2.x_ref), channel_id=1, source_target_pairs={{0,1},{1,2},{2,3},{4,5},{5,6},{6,7},{8,9},{9,10},{10,11},{12,13},{... | collective-permute-start | bytes 3145736 | tf_op jit(solution)/shard_map/ppermute | solution.py:247
  30.5 0.1 broadcast_in_dim.25.qcol_ref
  30.6 0.0 copy-start
  30.6 1.2 copy-done
  31.8 0.0 copy-start.2
  31.8 0.7 copy-done.2
  32.5 0.0 copy-start.3
  32.5 11.8 %own_part.2 = (bf16[512,1024]{1,0:T(8,128)(2,1)S(1)}, f32[512,1024]{1,0:T(8,128)S(1)}, f32[512,1024]{1,0:T(8,128)}) custom-call(bf16[512,1024]{1,0:T(8,128)(2,1)S(1)} %bitcast.15, f32[2,1024]{1,0:T(2,128)S(1)} %bitcast.18, bf16[4,1024,1024]{2,1,0:T(8,128)(2,1)} %bitcast.34, s32[512,128]{1,0:T(8,128)S(1)} %broadcast_in_dim.25.qcol_ref, ...), custom_call_target="tpu_custom_call" | custom-call | flops 7516192768 | bytes 12582912 | tf_op jit(solution)/shard_map/own_part/pallas_call | solution.py:155
  44.3 0.0 copy-done.3
  44.3 12.4 %piece_part.4 = (f32[512,1024]{1,0:T(8,128)S(1)}, f32[512,1024]{1,0:T(8,128)}) custom-call(bf16[512,1024]{1,0:T(8,128)(2,1)S(1)} %collective-permute-done.2.x_ref, f32[2,1024]{1,0:T(2,128)S(1)} %bitcast.19, bf16[4,1024,1024]{2,1,0:T(8,128)(2,1)} %bitcast.35, ...), custom_call_target="tpu_custom_call", output_to_operand_aliasing={{0}: (4, {}), {1}: (5, {})} | custom-call | flops 6442450944 | bytes 14680064 | tf_op jit(solution)/shard_map/piece_part/pallas_call | solution.py:186
  56.8 0.0 collective-permute-done.3.x_ref
  56.8 0.0 copy-start.1
  56.8 4.7 %piece_part.5 = (f32[512,1024]{1,0:T(8,128)S(1)}, f32[512,1024]{1,0:T(8,128)}) custom-call(bf16[512,1024]{1,0:T(8,128)(2,1)S(1)} %collective-permute-done.3.x_ref, f32[2,1024]{1,0:T(2,128)S(1)} %bitcast.20, bf16[4,1024,1024]{2,1,0:T(8,128)(2,1)} %bitcast.36, ...), custom_call_target="tpu_custom_call", output_to_operand_aliasing={{0}: (4, {}), {1}: (5, {})} | custom-call | flops 6442450944 | bytes 14680064 | tf_op jit(solution)/shard_map/piece_part/pallas_call | solution.py:186
  61.5 0.0 copy-done.1
  61.5 16.5 %finish_part.2 = bf16[512,1024]{1,0:T(8,128)(2,1)S(1)} custom-call(bf16[512,1024]{1,0:T(8,128)(2,1)S(1)} %bitcast.16, f32[512,1024]{1,0:T(8,128)S(1)} %get-tuple-element.24.num_ref, f32[512,1024]{1,0:T(8,128)} %get-tuple-element.25.den_ref, bf16[4,1024,1024]{2,1,0:T(8,128)(2,1)} %bitcast.37, f32[2,1024]{1,0:T(2,128)S(1)} %bitcast.21, ...), custom_call_target="tpu_custom_call" | custom-call | flops 9663676416 | bytes 25165824 | tf_op jit(solution)/shard_map/finish_part/pallas_call | solution.py:219
  78.0 0.0 copy-start.5
  78.0 0.0 collective-permute-done.4
  78.0 0.4 convert_subtract_fusion
  78.4 0.1 select_convert_fusion.1
  78.5 0.1 collective-permute-start.5
  78.6 0.1 copy-done.5
  78.7 0.4 collective-permute-start
  79.1 1.4 collective-permute-done
  80.5 0.0 collective-permute-done.5
  80.5 1.1 fusion.6
  81.6 1.5 collective-permute-start.6
  83.1 0.5 collective-permute-start.1
  83.6 12.2 %collective-permute-done.1 = f32[1,1024]{1,0:T(1,128)S(1)} collective-permute-done((f32[1,1024]{1,0:T(1,128)S(1)}, f32[1,1024]{1,0:T(1,128)S(1)}, u32[]{:S(2)}, u32[]{:S(2)}) %collective-permute-start.1) | collective-permute-done | bytes 4128 | tf_op jit(solution)/shard_map/ppermute | solution.py:251
  95.9 0.0 collective-permute-done.6
  95.9 1.2 fusion.4
  97.1 4.2 %collective-permute-start.7 = (bf16[256,1024]{1,0:T(8,128)(2,1)}, bf16[256,1024]{1,0:T(8,128)(2,1)}, u32[]{:S(2)}, u32[]{:S(2)}) collective-permute-start(bf16[256,1024]{1,0:T(8,128)(2,1)} %fusion.4), channel_id=1, source_target_pairs={{0,16},{4,20},{8,24},{12,28},{1,17},{5,21},{9,25},{13,29},{2,18},{... | collective-permute-start | bytes 1572872 | tf_op jit(solution)/shard_map/ppermute | solution.py:291
  101.3 10.1 %collective-permute-done.7 = bf16[256,1024]{1,0:T(8,128)(2,1)} collective-permute-done((bf16[256,1024]{1,0:T(8,128)(2,1)}, bf16[256,1024]{1,0:T(8,128)(2,1)}, u32[]{:S(2)}, u32[]{:S(2)}) %collective-permute-start.7) | collective-permute-done | bytes 524320 | tf_op jit(solution)/shard_map/ppermute | solution.py:291
  111.4 1.5 select_convert_fusion
  112.9 0.1 collective-permute-start.8
  113.0 1.9 collective-permute-done.8
  114.9 1.6 convert_select_fusion.2
  116.4 0.4 fusion.x_ref
  116.9 5.7 %collective-permute-start.9 = (bf16[512,1024]{1,0:T(8,128)(2,1)S(1)}, bf16[512,1024]{1,0:T(8,128)(2,1)S(1)}, u32[]{:S(2)}, u32[]{:S(2)}) collective-permute-start(bf16[512,1024]{1,0:T(8,128)(2,1)S(1)} %fusion.x_ref), channel_id=1, source_target_pairs={{0,1},{1,2},{2,3},{4,5},{5,6},{6,7},{8,9},{9,10},{10,11},{12,13},{... | collective-permute-start | bytes 3145736 | tf_op jit(solution)/shard_map/ppermute | solution.py:247
  122.5 22.7 %collective-permute-done.9.x_ref = bf16[512,1024]{1,0:T(8,128)(2,1)S(1)} collective-permute-done((bf16[512,1024]{1,0:T(8,128)(2,1)S(1)}, bf16[512,1024]{1,0:T(8,128)(2,1)S(1)}, u32[]{:S(2)}, u32[]{:S(2)}) %collective-permute-start.9) | collective-permute-done | bytes 1048608 | tf_op jit(solution)/shard_map/ppermute | solution.py:247
  145.2 4.4 %collective-permute-start.10 = (bf16[512,1024]{1,0:T(8,128)(2,1)S(1)}, bf16[512,1024]{1,0:T(8,128)(2,1)S(1)}, u32[]{:S(2)}, u32[]{:S(2)}) collective-permute-start(bf16[512,1024]{1,0:T(8,128)(2,1)S(1)} %collective-permute-done.9.x_ref), channel_id=1, source_target_pairs={{0,1},{1,2},{2,3},{4,5},{5,6},{6,7},{8,9},{9,10},{10,11},{12,13},{... | collective-permute-start | bytes 3145736 | tf_op jit(solution)/shard_map/ppermute | solution.py:247
  149.6 11.8 %own_part.3 = (bf16[512,1024]{1,0:T(8,128)(2,1)S(1)}, f32[512,1024]{1,0:T(8,128)S(1)}, f32[512,1024]{1,0:T(8,128)}) custom-call(bf16[512,1024]{1,0:T(8,128)(2,1)S(1)} %fusion.x_ref, f32[2,1024]{1,0:T(2,128)S(1)} %bitcast.22, bf16[4,1024,1024]{2,1,0:T(8,128)(2,1)} %bitcast.38, s32[512,128]{1,0:T(8,128)S(1)} %broadcast_in_dim.25.qcol_ref, ...), custom_call_target="tpu_custom_call" | custom-call | flops 7516192768 | bytes 12582912 | tf_op jit(solution)/shard_map/own_part/pallas_call | solution.py:155
  161.4 12.4 %piece_part.6 = (f32[512,1024]{1,0:T(8,128)S(1)}, f32[512,1024]{1,0:T(8,128)}) custom-call(bf16[512,1024]{1,0:T(8,128)(2,1)S(1)} %collective-permute-done.9.x_ref, f32[2,1024]{1,0:T(2,128)S(1)} %bitcast.23, bf16[4,1024,1024]{2,1,0:T(8,128)(2,1)} %bitcast.39, ...), custom_call_target="tpu_custom_call", output_to_operand_aliasing={{0}: (4, {}), {1}: (5, {})} | custom-call | flops 6442450944 | bytes 14680064 | tf_op jit(solution)/shard_map/piece_part/pallas_call | solution.py:186
  173.8 0.0 collective-permute-done.10.x_ref
  173.8 4.6 %piece_part.7 = (f32[512,1024]{1,0:T(8,128)S(1)}, f32[512,1024]{1,0:T(8,128)}) custom-call(bf16[512,1024]{1,0:T(8,128)(2,1)S(1)} %collective-permute-done.10.x_ref, f32[2,1024]{1,0:T(2,128)S(1)} %bitcast.24, bf16[4,1024,1024]{2,1,0:T(8,128)(2,1)} %bitcast.40, ...), custom_call_target="tpu_custom_call", output_to_operand_aliasing={{0}: (4, {}), {1}: (5, {})} | custom-call | flops 6442450944 | bytes 14680064 | tf_op jit(solution)/shard_map/piece_part/pallas_call | solution.py:186
  178.4 0.0 copy-start.4
  178.4 1.6 copy-done.4
  180.0 16.6 %finish_part.3 = bf16[512,1024]{1,0:T(8,128)(2,1)} custom-call(bf16[512,1024]{1,0:T(8,128)(2,1)S(1)} %fusion.x_ref, f32[512,1024]{1,0:T(8,128)S(1)} %get-tuple-element.31.num_ref, f32[512,1024]{1,0:T(8,128)S(1)} %copy-done.4, bf16[4,1024,1024]{2,1,0:T(8,128)(2,1)} %bitcast.41, f32[2,1024]{1,0:T(2,128)S(1)} %bitcast.25, bf16[1024,4096]{1,0:T(8,128)(2,1)} %bitcast.43, ...), custom_call_target="tpu_custom_call" | custom-call | flops 9663676416 | bytes 25165824 | tf_op jit(solution)/shard_map/finish_part/pallas_call | solution.py:219
  (2 shorter events, 0.0 us)
Async XLA Ops:
  0.0 27.0 %collective-permute-start.2 = (bf16[512,1024]{1,0:T(8,128)(2,1)}, bf16[512,1024]{1,0:T(8,128)(2,1)S(1)}, u32[]{:S(2)}, u32[]{:S(2)}) collective-permute-start(bf16[512,1024]{1,0:T(8,128)(2,1)} %bitcast.13), channel_id=1, source_target_pairs={{0,1},{1,2},{2,3},{4,5},{5,6},{6,7},{8,9},{9,10},{10,11},{12,13},{... | collective-permute-start | bytes 3145736 | tf_op jit(solution)/shard_map/ppermute | solution.py:247
  3.5 74.5 %collective-permute-start.4 = (bf16[512,1024]{1,0:T(8,128)(2,1)}, bf16[512,1024]{1,0:T(8,128)(2,1)S(1)}, u32[]{:S(2)}, u32[]{:S(2)}) collective-permute-start(bf16[512,1024]{1,0:T(8,128)(2,1)} %bitcast.14), channel_id=1, source_target_pairs={{4,0},{8,4},{12,8},{16,12},{20,16},{24,20},{28,24},{5,1},{9,5},{13... | collective-permute-start | bytes 3145736 | tf_op jit(solution)/shard_map/ppermute | solution.py:247
  27.0 29.8 %collective-permute-start.3 = (bf16[512,1024]{1,0:T(8,128)(2,1)S(1)}, bf16[512,1024]{1,0:T(8,128)(2,1)S(1)}, u32[]{:S(2)}, u32[]{:S(2)}) collective-permute-start(bf16[512,1024]{1,0:T(8,128)(2,1)S(1)} %collective-permute-done.2.x_ref), channel_id=1, source_target_pairs={{0,1},{1,2},{2,3},{4,5},{5,6},{6,7},{8,9},{9,10},{10,11},{12,13},{... | collective-permute-start | bytes 3145736 | tf_op jit(solution)/shard_map/ppermute | solution.py:247
  30.6 1.2 copy-start
  31.8 0.7 copy-start.2
  32.5 11.8 %copy-start.3 = (f32[1,1,2,1024]{3,2,1,0:T(2,128)S(1)}, f32[1,1,2,1024]{3,2,1,0:T(2,128)}, u32[]{:S(2)}) copy-start(f32[1,1,2,1024]{3,2,1,0:T(2,128)} %param.12) | copy-start | bytes 24580
  56.8 4.7 %copy-start.1 = (bf16[1,1,512,1024]{3,2,1,0:T(8,128)(2,1)S(1)}, bf16[1,1,512,1024]{3,2,1,0:T(8,128)(2,1)}, u32[]{:S(2)}) copy-start(bf16[1,1,512,1024]{3,2,1,0:T(8,128)(2,1)} %param.7) | copy-start | bytes 3145732
  78.0 0.7 copy-start.5
  78.5 2.0 %collective-permute-start.5 = (bf16[256,1024]{1,0:T(8,128)(2,1)S(1)}, bf16[256,1024]{1,0:T(8,128)(2,1)S(1)}, u32[]{:S(2)}, u32[]{:S(2)}) collective-permute-start(bf16[256,1024]{1,0:T(8,128)(2,1)S(1)} %select_convert_fusion.1), channel_id=1, source_target_pairs={{0,4},{4,0},{8,12},{12,8},{16,20},{20,16},{24,28},{28,24},{1,5},{5... | collective-permute-start | bytes 1572872 | tf_op jit(solution)/shard_map/ppermute | solution.py:251
  78.7 1.8 collective-permute-start
  81.6 14.3 %collective-permute-start.6 = (bf16[256,1024]{1,0:T(8,128)(2,1)}, bf16[256,1024]{1,0:T(8,128)(2,1)S(1)}, u32[]{:S(2)}, u32[]{:S(2)}) collective-permute-start(bf16[256,1024]{1,0:T(8,128)(2,1)} %get-tuple-element.36), channel_id=1, source_target_pairs={{0,8},{4,12},{8,0},{12,4},{16,24},{20,28},{24,16},{28,20},{1,9},{5... | collective-permute-start | bytes 1572872 | tf_op jit(solution)/shard_map/ppermute | solution.py:251
  83.1 12.7 %collective-permute-start.1 = (f32[1,1024]{1,0:T(1,128)S(1)}, f32[1,1024]{1,0:T(1,128)S(1)}, u32[]{:S(2)}, u32[]{:S(2)}) collective-permute-start(f32[1,1024]{1,0:T(1,128)S(1)} %get-tuple-element.33), channel_id=1, source_target_pairs={{0,8},{4,12},{8,0},{12,4},{16,24},{20,28},{24,16},{28,20},{1,9},{5... | collective-permute-start | bytes 12296 | tf_op jit(solution)/shard_map/ppermute | solution.py:251
  97.1 14.4 %collective-permute-start.7 = (bf16[256,1024]{1,0:T(8,128)(2,1)}, bf16[256,1024]{1,0:T(8,128)(2,1)}, u32[]{:S(2)}, u32[]{:S(2)}) collective-permute-start(bf16[256,1024]{1,0:T(8,128)(2,1)} %fusion.4), channel_id=1, source_target_pairs={{0,16},{4,20},{8,24},{12,28},{1,17},{5,21},{9,25},{13,29},{2,18},{... | collective-permute-start | bytes 1572872 | tf_op jit(solution)/shard_map/ppermute | solution.py:291
  112.9 2.0 %collective-permute-start.8 = (bf16[256,1024]{1,0:T(8,128)(2,1)S(1)}, bf16[256,1024]{1,0:T(8,128)(2,1)S(1)}, u32[]{:S(2)}, u32[]{:S(2)}) collective-permute-start(bf16[256,1024]{1,0:T(8,128)(2,1)S(1)} %select_convert_fusion), channel_id=1, source_target_pairs={{0,4},{4,0},{8,12},{12,8},{16,20},{20,16},{24,28},{28,24},{1,5},{5... | collective-permute-start | bytes 1572872 | tf_op jit(solution)/shard_map/ppermute | solution.py:251
  116.9 28.4 %collective-permute-start.9 = (bf16[512,1024]{1,0:T(8,128)(2,1)S(1)}, bf16[512,1024]{1,0:T(8,128)(2,1)S(1)}, u32[]{:S(2)}, u32[]{:S(2)}) collective-permute-start(bf16[512,1024]{1,0:T(8,128)(2,1)S(1)} %fusion.x_ref), channel_id=1, source_target_pairs={{0,1},{1,2},{2,3},{4,5},{5,6},{6,7},{8,9},{9,10},{10,11},{12,13},{... | collective-permute-start | bytes 3145736 | tf_op jit(solution)/shard_map/ppermute | solution.py:247
  145.2 28.6 %collective-permute-start.10 = (bf16[512,1024]{1,0:T(8,128)(2,1)S(1)}, bf16[512,1024]{1,0:T(8,128)(2,1)S(1)}, u32[]{:S(2)}, u32[]{:S(2)}) collective-permute-start(bf16[512,1024]{1,0:T(8,128)(2,1)S(1)} %collective-permute-done.9.x_ref), channel_id=1, source_target_pairs={{0,1},{1,2},{2,3},{4,5},{5,6},{6,7},{8,9},{9,10},{10,11},{12,13},{... | collective-permute-start | bytes 3145736 | tf_op jit(solution)/shard_map/ppermute | solution.py:247
  178.4 1.6 copy-start.4
